TPU v7x, 32 devices: a whole 2x2x4 slice. The times are simulated.
32 devices in a mesh: sub: 16 (over z, y, x), grp: 2 (over core).
Axes of the slice: x: 2, y: 2, z: 4, core: 2. Of those that a mesh axis runs over, the one named last changes fastest.
Arguments:
- rhs_jump: float32 [16, 2, 256, 256], P('sub', 'grp'), may hold values from -6 to 6
- incision: int32 [16, 2, 256], P('sub', 'grp'), may hold values 0 or 1
- precond: float32 [16, 2, 256], P('sub', 'grp'), may hold values from 0.5 to 2
- left_rows: int32 [16, 2, 256], P('sub', 'grp'), may hold values from 0 to 1151, as said below
- right_rows: int32 [16, 2, 256], P('sub', 'grp'), may hold values from 0 to 1151, as said below
- diag_inv: float32 [16, 2, 3, 384, 384], P('sub', 'grp'), as said below
- coupling: float32 [16, 2, 2, 384, 384], P('sub', 'grp'), may hold values from -0.09185587 to 0.09185587
- coarse_basis: float32 [16, 2, 3, 384, 128], P('sub', 'grp'), may hold values from -0.25 to 0.25
- coarse_inv: float32 [16, 128, 128], P('sub'), as said below
Outputs:
- multipliers: float32 [16, 2, 256, 256], P('sub', 'grp')
- residual: float32 [16, 2, 256, 256], P('sub', 'grp')
Inputs may be any that keep to these rules, and one draw needn't show every extreme that they name: `left_rows`: for each subdomain, its 256 left rows and 256 right rows are 512 distinct interior rows. `right_rows`: see left_rows. `diag_inv`: every block is invertible. `coarse_inv`: every block is symmetric positive definite.
All inputs are finite; a program needn't handle non-finite values. No bound on the sum of `incision` on one device may be relied on, other than what follows from the above.
Results may differ from a plain program's by a relative error of at most 0.0003.
Values sent between devices are 32-bit elements; how exact they have to be, the bound alone decides.
A program may use at most 64 MiB of HBM per device.

v0:
```python
import jax
import jax.numpy as jnp
from jax import lax
from jax.sharding import PartitionSpec as P

ITERS = 3


HIGH = lax.Precision.HIGHEST


def passed_along(shard, axis, by):
    peers = lax.axis_size(axis)
    return lax.ppermute(shard, axis, [(i, (i + by) % peers) for i in range(peers)])


def pair_totals(first, second):
    return lax.psum((first, second), ("sub", "grp"))


def local(
    rhs_jump, incision, precond, left_rows, right_rows, diag_inv, coupling, coarse_basis, coarse_inv
):
    load_rhs = rhs_jump[0, 0]
    cut = incision[0, 0].astype(jnp.float32)[:, None]
    scaling = precond[0, 0][:, None]
    lrow = left_rows[0, 0]
    rrow = right_rows[0, 0]
    dinv = diag_inv[0, 0]
    coup = coupling[0, 0]
    nblk, blk = (dinv.shape[0], dinv.shape[1])
    order = nblk * blk
    basis = coarse_basis[0, 0].reshape(order, -1)
    cinv = coarse_inv[0]
    width = load_rhs.shape[1]

    def banded(load):
        pieces = load.reshape(nblk, blk, width)
        forward = []
        for block in range(nblk):
            rhs_now = pieces[block]
            if block > 0:
                rhs_now = rhs_now - jnp.dot(coup[block - 1], forward[-1], precision=HIGH)
            forward.append(jnp.dot(dinv[block], rhs_now, precision=HIGH))
        backward = [None] * nblk
        for block in range(nblk - 1, -1, -1):
            rhs_now = forward[block]
            if block < nblk - 1:
                rhs_now = rhs_now - jnp.dot(coup[block].T, backward[block + 1], precision=HIGH)
            backward[block] = jnp.dot(dinv[block].T, rhs_now, precision=HIGH)
        return jnp.concatenate(backward, axis=0)

    def interior(own, left):
        zeros = jnp.zeros((order, width), jnp.float32)
        load = zeros.at[rrow].add(own).at[lrow].add(-left)
        primal = jnp.einsum("np,nr->pr", basis, load, precision=HIGH)
        summed = lax.psum(primal, "grp")
        solved = banded(load)
        coarse = jnp.dot(cinv, summed, precision=HIGH)
        disp = solved + jnp.dot(basis, coarse, precision=HIGH)
        return (jnp.take(disp, lrow, axis=0), jnp.take(disp, rrow, axis=0))

    start = load_rhs[None]
    scales = scaling[None]
    cuts = cut[None]

    def apply(stack):
        own = stack[0]
        left = passed_along(own, "sub", 1)
        yleft, yright = interior(own, left)
        nextone = passed_along(yleft, "sub", -1)
        return (cut * (yright - nextone))[None]

    def local_dot(first, second):
        return jnp.sum(first[-1] * second[-1], axis=0)

    multipliers = jnp.zeros_like(start)
    residual = cuts * start
    zvec = scales * residual
    image = apply(zvec)
    rz_now, curve = pair_totals(local_dot(residual, zvec), local_dot(image, zvec))
    alpha = rz_now / curve
    direc, along = (zvec, image)
    for step in range(ITERS):
        multipliers = multipliers + alpha * direc
        residual = residual - alpha * along
        if step + 1 < ITERS:
            zvec = scales * residual
            image = apply(zvec)
            rz_new, curve = pair_totals(local_dot(residual, zvec), local_dot(image, zvec))
            ratio = rz_new / rz_now
            alpha = rz_new / (curve - ratio * rz_new / alpha)
            direc = zvec + ratio * direc
            along = image + ratio * along
            rz_now = rz_new
    return (multipliers[-1][None, None], residual[-1][None, None])


def solution(mesh):
    placed = (
        P("sub", "grp", None, None),
        P("sub", "grp", None),
        P("sub", "grp", None),
        P("sub", "grp", None),
        P("sub", "grp", None),
        P("sub", "grp", None, None, None),
        P("sub", "grp", None, None, None),
        P("sub", "grp", None, None, None),
        P("sub", None, None),
    )
    return jax.shard_map(
        local,
        mesh=mesh,
        in_specs=placed,
        out_specs=(P("sub", "grp", None, None), P("sub", "grp", None, None)),
        check_vma=False,
    )
```

profile of v0, /device:TPU:0, one launch (start us, length us, event | category | flops | bytes accessed | tf_op | source)
XLA Modules:
  0.0 362.4 jit_solution(6969571927782280861)
XLA Ops:
  14.8 3.6 %scatter_custom_fusion = f32[1152,256]{1,0:T(8,128)} fusion(s32[256]{0:T(256)S(1)} %bitcast.217, f32[]{:T(128)} %constant.1.clone.1, f32[1,1,256,256]{3,2,1,0:T(8,128)} %param.11, f32[256]{0:T(256)} %bitcast.194, f32[256]{0:T(256)S(1)} %bitcast.204), kind=kCustom, calls=%fused_computation.85 | custom fusion | flops 196608 | bytes 1443844 | tf_op jit(solution)/shard_map/scatter-add | solution.py:55
  19.0 3.3 collective-permute-done
  23.1 4.7 %scatter_custom_fusion.1 = f32[1152,256]{1,0:T(8,128)} fusion(f32[1152,256]{1,0:T(8,128)} %scatter_custom_fusion, s32[256]{0:T(256)S(1)} %bitcast.214, f32[256,256]{1,0:T(8,128)} %copy-done.23), kind=kCustom, calls=%fused_computation.147 | custom fusion | flops 131072 | bytes 1441792 | tf_op jit(solution)/shard_map/scatter-add | solution.py:55
  45.0 12.7 %all-reduce.7.cloned.1.call-done = f32[128,256]{0,1:T(8,128)} async-done(((f32[128,256]{0,1:T(8,128)}), f32[128,256]{0,1:T(8,128)}) %all-reduce.7.cloned.1.call-update) | async-done | bytes 131088 | tf_op jit(solution)/shard_map/psum | solution.py:57
  58.8 3.3 fusion.2
  69.5 5.4 %collective-permute-start.1 = (f32[256,256]{1,0:T(8,128)}, f32[256,256]{1,0:T(8,128)}, u32[]{:S(2)}, u32[]{:S(2)}) collective-permute-start(f32[256,256]{1,0:T(8,128)} %broadcast_select_fusion.2), channel_id=1, source_target_pairs={{0,30},{2,0},{4,2},{6,4},{8,6},{10,8},{12,10},{14,12},{16,14},{18,... | collective-permute-start | bytes 786440 | tf_op jit(solution)/shard_map/ppermute | solution.py:14
  83.8 40.7 %all-reduce.2 = (f32[256]{0:T(256)}, f32[256]{0:T(256)}) all-reduce(f32[256]{0:T(256)} %get-tuple-element.4, f32[256]{0:T(256)} %get-tuple-element.3), channel_id=1, replica_groups=mesh['sub'=16,'grp'=2] {'sub','grp'}, use_global_device_ids=true, to_apply=%region_1.0 | all-reduce | flops 512 | bytes 4096 | tf_op jit(solution)/shard_map/psum | solution.py:18
  130.0 3.5 scatter_custom_fusion.2
  133.5 5.6 %collective-permute-done.2 = f32[256,256]{1,0:T(8,128)} collective-permute-done((f32[256,256]{1,0:T(8,128)}, f32[256,256]{1,0:T(8,128)}, u32[]{:S(2)}, u32[]{:S(2)}) %collective-permute-start.2) | collective-permute-done | bytes 262176 | tf_op jit(solution)/shard_map/ppermute | solution.py:14
  139.1 4.9 %scatter_custom_fusion.3 = f32[1152,256]{1,0:T(8,128)} fusion(f32[1152,256]{1,0:T(8,128)} %scatter_custom_fusion.2, s32[256]{0:T(256)} %bitcast.215, f32[256,256]{1,0:T(8,128)} %collective-permute-done.2), kind=kCustom, calls=%fused_computation.142 | custom fusion | flops 131072 | bytes 1441792 | tf_op jit(solution)/shard_map/scatter-add | solution.py:55
  144.0 3.3 fusion.43
  163.7 12.1 %all-reduce.9.cloned.1.call-done = f32[128,256]{0,1:T(8,128)} async-done(((f32[128,256]{0,1:T(8,128)}), f32[128,256]{0,1:T(8,128)}) %all-reduce.9.cloned.1.call-update) | async-done | bytes 131088 | tf_op jit(solution)/shard_map/psum | solution.py:57
  177.0 3.3 fusion.1
  187.7 5.4 %collective-permute-start.3 = (f32[256,256]{1,0:T(8,128)}, f32[256,256]{1,0:T(8,128)}, u32[]{:S(2)}, u32[]{:S(2)}) collective-permute-start(f32[256,256]{1,0:T(8,128)} %broadcast_select_fusion.1), channel_id=1, source_target_pairs={{0,30},{2,0},{4,2},{6,4},{8,6},{10,8},{12,10},{14,12},{16,14},{18,... | collective-permute-start | bytes 786440 | tf_op jit(solution)/shard_map/ppermute | solution.py:14
  196.0 3.4 collective-permute-done.3
  202.0 40.8 %all-reduce.1 = (f32[256]{0:T(256)}, f32[256]{0:T(256)}) all-reduce(f32[256]{0:T(256)} %get-tuple-element.8, f32[256]{0:T(256)} %get-tuple-element.7), channel_id=1, replica_groups=mesh['sub'=16,'grp'=2] {'sub','grp'}, use_global_device_ids=true, to_apply=%region_8.10 | all-reduce | flops 512 | bytes 4096 | tf_op jit(solution)/shard_map/psum | solution.py:18
  248.8 3.5 scatter_custom_fusion.4
  252.3 5.6 %collective-permute-done.4 = f32[256,256]{1,0:T(8,128)} collective-permute-done((f32[256,256]{1,0:T(8,128)}, f32[256,256]{1,0:T(8,128)}, u32[]{:S(2)}, u32[]{:S(2)}) %collective-permute-start.4) | collective-permute-done | bytes 262176 | tf_op jit(solution)/shard_map/ppermute | solution.py:14
  257.9 4.7 %scatter_custom_fusion.5 = f32[1152,256]{1,0:T(8,128)} fusion(f32[1152,256]{1,0:T(8,128)} %scatter_custom_fusion.4, s32[256]{0:T(256)} %bitcast.216, f32[256,256]{1,0:T(8,128)} %collective-permute-done.4), kind=kCustom, calls=%fused_computation.136 | custom fusion | flops 131072 | bytes 1441792 | tf_op jit(solution)/shard_map/scatter-add | solution.py:55
  262.6 3.3 fusion.40
  282.4 12.0 %all-reduce.11.cloned.1.call-done = f32[128,256]{0,1:T(8,128)} async-done(((f32[128,256]{0,1:T(8,128)}), f32[128,256]{0,1:T(8,128)}) %all-reduce.11.cloned.1.call-update) | async-done | bytes 131088 | tf_op jit(solution)/shard_map/psum | solution.py:57
  300.1 5.5 %collective-permute-start.5 = (f32[256,256]{1,0:T(8,128)}, f32[256,256]{1,0:T(8,128)}, u32[]{:S(2)}, u32[]{:S(2)}) collective-permute-start(f32[256,256]{1,0:T(8,128)} %broadcast_select_fusion), channel_id=1, source_target_pairs={{0,30},{2,0},{4,2},{6,4},{8,6},{10,8},{12,10},{14,12},{16,14},{18,... | collective-permute-start | bytes 786440 | tf_op jit(solution)/shard_map/ppermute | solution.py:14
  306.5 5.4 %collective-permute-done.5 = f32[256,256]{1,0:T(8,128)} collective-permute-done((f32[256,256]{1,0:T(8,128)}, f32[256,256]{1,0:T(8,128)}, u32[]{:S(2)}, u32[]{:S(2)}) %collective-permute-start.5) | collective-permute-done | bytes 262176 | tf_op jit(solution)/shard_map/ppermute | solution.py:14
  313.0 40.5 %all-reduce = (f32[256]{0:T(256)S(1)}, f32[256]{0:T(256)S(1)}) all-reduce(f32[256]{0:T(256)S(1)} %get-tuple-element.6, f32[256]{0:T(256)S(1)} %get-tuple-element.5), channel_id=1, replica_groups=mesh['sub'=16,'grp'=2] {'sub','grp'}, use_global_device_ids=true, to_apply=%region_15.17 | all-reduce | flops 512 | bytes 4096 | tf_op jit(solution)/shard_map/psum | solution.py:18
  (154 shorter events, 111.2 us)
Async XLA Ops:
  7.2 32.2 %copy-start = (f32[1,1,3,384,128]{4,3,2,1,0:T(8,128)S(1)}, f32[1,1,3,384,128]{4,3,2,1,0:T(8,128)}, u32[]{:S(2)}) copy-start(f32[1,1,3,384,128]{4,3,2,1,0:T(8,128)} %param.18) | copy-start | bytes 1769476
  7.2 50.5 %all-reduce.7.cloned.1.call-start = ((), (), s32[]{:S(2)}) async-start(), calls=%async_computation | async-start | bytes 262144 | tf_op jit(solution)/shard_map/psum | solution.py:57
  9.1 13.3 %collective-permute-start = (f32[256,256]{1,0:T(8,128)S(1)}, f32[256,256]{1,0:T(8,128)S(1)}, u32[]{:S(2)}, u32[]{:S(2)}) collective-permute-start(f32[256,256]{1,0:T(8,128)S(1)} %fusion.96), channel_id=1, source_target_pairs={{0,2},{2,4},{4,6},{6,8},{8,10},{10,12},{12,14},{14,16},{16,18},{18... | collective-permute-start | bytes 786440 | tf_op jit(solution)/shard_map/ppermute | solution.py:14
  12.7 15.1 %copy-start.37 = (s32[256,1]{0,1:T(1,128)}, s32[256,1]{0,1:T(1,128)S(1)}, u32[]{:S(2)}) copy-start(s32[256,1]{0,1:T(1,128)S(1)} %compare_select_fusion) | copy-start | bytes 3076
  14.1 53.7 %copy-start.32 = (pred[256]{0:T(512)(128)(4,1)}, pred[256]{0:T(512)(128)(4,1)S(1)}, u32[]{:S(2)}) copy-start(pred[256]{0:T(512)(128)(4,1)S(1)} %compare_and_fusion) | copy-start | bytes 772
  14.8 13.0 %copy-start.1 = (f32[1,1,3,384,384]{4,3,2,1,0:T(8,128)S(1)}, f32[1,1,3,384,384]{4,3,2,1,0:T(8,128)}, u32[]{:S(2)}) copy-start(f32[1,1,3,384,384]{4,3,2,1,0:T(8,128)} %param.16) | copy-start | bytes 5308420
  42.1 133.7 %all-reduce.9.cloned.1.call-start = ((), (), s32[]{:S(2)}) async-start(), calls=%async_computation.1 | async-start | bytes 262144 | tf_op jit(solution)/shard_map/psum | solution.py:57
  69.5 11.7 %collective-permute-start.1 = (f32[256,256]{1,0:T(8,128)}, f32[256,256]{1,0:T(8,128)}, u32[]{:S(2)}, u32[]{:S(2)}) collective-permute-start(f32[256,256]{1,0:T(8,128)} %broadcast_select_fusion.2), channel_id=1, source_target_pairs={{0,30},{2,0},{4,2},{6,4},{8,6},{10,8},{12,10},{14,12},{16,14},{18,... | collective-permute-start | bytes 786440 | tf_op jit(solution)/shard_map/ppermute | solution.py:14
  127.7 11.4 %collective-permute-start.2 = (f32[256,256]{1,0:T(8,128)}, f32[256,256]{1,0:T(8,128)}, u32[]{:S(2)}, u32[]{:S(2)}) collective-permute-start(f32[256,256]{1,0:T(8,128)} %get-tuple-element.23), channel_id=1, source_target_pairs={{0,2},{2,4},{4,6},{6,8},{8,10},{10,12},{12,14},{14,16},{16,18},{18... | collective-permute-start | bytes 786440 | tf_op jit(solution)/shard_map/ppermute | solution.py:14
  160.8 133.6 %all-reduce.11.cloned.1.call-start = ((), (), s32[]{:S(2)}) async-start(), calls=%async_computation.2 | async-start | bytes 262144 | tf_op jit(solution)/shard_map/psum | solution.py:57
  187.7 11.7 %collective-permute-start.3 = (f32[256,256]{1,0:T(8,128)}, f32[256,256]{1,0:T(8,128)}, u32[]{:S(2)}, u32[]{:S(2)}) collective-permute-start(f32[256,256]{1,0:T(8,128)} %broadcast_select_fusion.1), channel_id=1, source_target_pairs={{0,30},{2,0},{4,2},{6,4},{8,6},{10,8},{12,10},{14,12},{16,14},{18,... | collective-permute-start | bytes 786440 | tf_op jit(solution)/shard_map/ppermute | solution.py:14
  246.5 11.4 %collective-permute-start.4 = (f32[256,256]{1,0:T(8,128)}, f32[256,256]{1,0:T(8,128)}, u32[]{:S(2)}, u32[]{:S(2)}) collective-permute-start(f32[256,256]{1,0:T(8,128)} %get-tuple-element.17), channel_id=1, source_target_pairs={{0,2},{2,4},{4,6},{6,8},{8,10},{10,12},{12,14},{14,16},{16,18},{18... | collective-permute-start | bytes 786440 | tf_op jit(solution)/shard_map/ppermute | solution.py:14
  279.4 15.0 %copy-start.22 = (f32[1,128,128]{2,1,0:T(8,128)S(1)}, f32[1,128,128]{2,1,0:T(8,128)}, u32[]{:S(2)}) copy-start(f32[1,128,128]{2,1,0:T(8,128)} %param.19) | copy-start | bytes 196612
  279.4 16.2 %copy-start.16 = (f32[256,384]{1,0:T(8,128)S(1)}, f32[256,384]{1,0:T(8,128)}, u32[]{:S(2)}) copy-start(f32[256,384]{1,0:T(8,128)} %copy-done.15) | copy-start | bytes 1179652
  300.0 53.6 %copy-start.35 = (f32[256]{0:T(256)S(1)}, f32[256]{0:T(256)}, u32[]{:S(2)}) copy-start(f32[256]{0:T(256)} %get-tuple-element.11) | copy-start | bytes 3076
  300.0 53.6 %copy-start.36 = (f32[256]{0:T(256)S(1)}, f32[256]{0:T(256)}, u32[]{:S(2)}) copy-start(f32[256]{0:T(256)} %get-tuple-element.20) | copy-start | bytes 3076
  300.0 53.6 %copy-start.8 = (f32[1,1,256,256]{3,2,1,0:T(8,128)S(1)}, f32[1,1,256,256]{3,2,1,0:T(8,128)}, u32[]{:S(2)}) copy-start(f32[1,1,256,256]{3,2,1,0:T(8,128)} %param.11) | copy-start | bytes 786436
  300.0 53.6 %copy-start.9 = (f32[256,256]{1,0:T(8,128)S(1)}, f32[256,256]{1,0:T(8,128)}, u32[]{:S(2)}) copy-start(f32[256,256]{1,0:T(8,128)} %get-tuple-element.24) | copy-start | bytes 786436
  300.0 53.6 %copy-start.10 = (f32[256,256]{1,0:T(8,128)S(1)}, f32[256,256]{1,0:T(8,128)}, u32[]{:S(2)}) copy-start(f32[256,256]{1,0:T(8,128)} %get-tuple-element.25) | copy-start | bytes 786436
  300.1 53.6 %copy-start.21 = (f32[256,256]{1,0:T(8,128)S(1)}, f32[256,256]{1,0:T(8,128)}, u32[]{:S(2)}) copy-start(f32[256,256]{1,0:T(8,128)} %get-tuple-element.22) | copy-start | bytes 786436
  300.1 53.6 %copy-start.26 = (f32[256]{0:T(256)S(1)}, f32[256]{0:T(256)}, u32[]{:S(2)}) copy-start(f32[256]{0:T(256)} %copy-done.25) | copy-start | bytes 3076
  300.1 53.6 %copy-start.28 = (f32[256]{0:T(256)S(1)}, f32[256]{0:T(256)}, u32[]{:S(2)}) copy-start(f32[256]{0:T(256)} %copy-done.27) | copy-start | bytes 3076
  300.1 53.6 %copy-start.30 = (f32[256]{0:T(256)S(1)}, f32[256]{0:T(256)}, u32[]{:S(2)}) copy-start(f32[256]{0:T(256)} %copy-done.29) | copy-start | bytes 3076
  300.1 11.8 %collective-permute-start.5 = (f32[256,256]{1,0:T(8,128)}, f32[256,256]{1,0:T(8,128)}, u32[]{:S(2)}, u32[]{:S(2)}) collective-permute-start(f32[256,256]{1,0:T(8,128)} %broadcast_select_fusion), channel_id=1, source_target_pairs={{0,30},{2,0},{4,2},{6,4},{8,6},{10,8},{12,10},{14,12},{16,14},{18,... | collective-permute-start | bytes 786440 | tf_op jit(solution)/shard_map/ppermute | solution.py:14
  (24 other events, 87.4 us)
Sparse Core Ops, SparseCore 0:
  42.2 15.4 all-reduce.6
  160.9 14.8 all-reduce.8
  279.6 14.8 all-reduce.10
where the time goes:
time: 367 us; the launch traced here: 362 us
  blocking collectives  122 us (33%)
  matrix products  66.7 us (18%)
  waiting for transfers between devices  61.8 us (17%)
  other arithmetic  50.2 us (14%)
  starting transfers between devices  24.3 us (7%)
  local copies, waits for them, and re-layouts  22.8 us (6%)
  between operations  14.6 us (4%)
    psum x3, blocking collectives, pair_totals(): return lax.psum((first, second), ('sub', 'grp'))  122 us
    psum x3, waiting for transfers between devices, interior(): summed = lax.psum(primal, 'grp')  36.8 us
    ppermute x6, waiting for transfers between devices, passed_along(): lax.ppermute(shard, axis, [(i, (i + by) % peers) for i in range(peers)])  24.9 us
    scatter-add x6, other arithmetic, interior(): load = zeros.at[rrow].add(own).at[lrow].add(-left)  24.9 us
    ppermute x6, starting transfers between devices, passed_along(): lax.ppermute(shard, axis, [(i, (i + by) % peers) for i in range(peers)])  23.8 us
    dot_general x9, matrix products, banded(): forward.append(jnp.dot(dinv[block], rhs_now, precision=HIGH))  17.9 us
    dot_general x9, matrix products, banded(): backward[block] = jnp.dot(dinv[block].T, rhs_now, precision=HIGH)  13.7 us
    gather x6, local copies, waits for them, and re-layouts, interior(): return (jnp.take(disp, lrow, axis=0), jnp.take(disp, rrow, axis=0))  13.7 us
  transfers between devices with their start and end apart: 9, of which 9 were waited for; matrix products, arithmetic and copies ran while one was open for 9% of the time, Pallas kernels for 0%

commit v1 on v0

v1 whole, which is shorter than its diff:
```python
import functools

import jax
import jax.numpy as jnp
from jax import lax
from jax.experimental import pallas as pl
from jax.experimental.pallas import tpu as pltpu
from jax.sharding import PartitionSpec as P

ROUNDS = 3
MESH = pl.DeviceIdType.MESH
F32 = jnp.float32
BF16 = jnp.bfloat16


def split(x):
    high = x.astype(BF16)
    return high, (x - high.astype(F32)).astype(BF16)


def dot(a, b, ca=1, cb=0):
    return lax.dot_general(a, b, (((ca,), (cb,)), ((), ())), preferred_element_type=F32)


def dot3(a, b, ca=1, cb=0):
    (ah, al), (bh, bl) = a, b
    return dot(ah, bh, ca, cb) + (dot(ah, bl, ca, cb) + dot(al, bh, ca, cb))


def kernel(
    subs, grps, inner, chunks,
    rhs, cut_in, pre_in, lrow, rrow, dinv, coup, basis, cinv,
    mult, resid,
    v0, w0, v2, upper, cuts, pres, smat, bet, bc, gmat,
    ysend, yrecv, usend, urecv, dsend, drecv, red, reda, redb, redm,
    s_v0, r_v0, s_cm, r_cm, s_up, r_up, s_dn, r_dn, s_u, r_u, s_a, r_a, s_b, r_b,
):
    sub, grp = lax.axis_index("sub"), lax.axis_index("grp")
    width = rhs.shape[0]
    cols = rhs.shape[1] // chunks
    nblk, blk = dinv.shape[0], dinv.shape[1]
    after = (lax.rem(sub + 1, subs), grp)
    before = (lax.rem(sub + subs - 1, subs), grp)
    plane = inner * grps
    outer = subs // inner
    at_plane = lax.rem(sub, inner) * grps + grp
    base = lax.div(sub, inner) * inner

    def plane_peer(j):
        idx = lax.rem(at_plane + j, plane)
        return (base + lax.div(idx, grps), lax.rem(idx, grps))

    def outer_peer(j):
        return (lax.rem(base + j * inner, subs) + lax.rem(sub, inner), grp)

    def grp_peer(j):
        return (sub, lax.rem(grp + j, grps))

    peers = [after, before]
    peers += [plane_peer(j) for j in range(1, plane)]
    peers += [outer_peer(j) for j in range(1, outer)]
    barrier = pltpu.get_barrier_semaphore()
    for peer in peers:
        pl.semaphore_signal(barrier, inc=1, device_id=peer, device_id_type=MESH)

    def send(src, dst, ssem, rsem, peer):
        copy = pltpu.make_async_remote_copy(
            src_ref=src, dst_ref=dst, send_sem=ssem, recv_sem=rsem, device_id=peer, device_id_type=MESH
        )
        copy.start()
        return copy

    def col(c):
        return slice(c * cols, (c + 1) * cols)

    eye = lax.broadcasted_iota(jnp.int32, (width, width), 0) == lax.broadcasted_iota(
        jnp.int32, (width, width), 1
    )

    def column(row):
        return jnp.broadcast_to(
            jnp.sum(jnp.where(eye, row, 0.0), axis=1, keepdims=True), (width, cols)
        )

    cut_row = cut_in[...].astype(F32)
    dsend[0:1, :] = cut_row
    dsend[1:2, :] = pre_in[...]
    cuts[:width, :] = column(cut_row)
    pres[:width, :] = column(pre_in[...])
    for c in range(chunks):
        v0[c, :width, :] = pres[:width, :] * (cuts[:width, :] * rhs[:, col(c)])
    pl.semaphore_wait(barrier, len(peers))
    sent = []
    cm_copy = send(dsend, drecv, s_cm, r_cm, after)
    v0_copy = [
        send(v0.at[c, pl.ds(0, width)], v0.at[c, pl.ds(width, width)], s_v0.at[c], r_v0.at[c], after)
        for c in range(chunks)
    ]
    sent += [cm_copy] + v0_copy

    index = jnp.concatenate([rrow[...], lrow[...]], axis=1)
    sign = jnp.where(
        lax.broadcasted_iota(jnp.int32, (1, 2 * width), 1) < width, 1.0, -1.0
    ).astype(F32)

    def chosen(k):
        rows = lax.broadcasted_iota(jnp.int32, (blk, 2 * width), 0) + k * blk
        return jnp.where(rows == index, sign, 0.0)

    total = None
    for k in range(nblk):
        pick = chosen(k)
        pick16 = pick.astype(BF16)
        bh, bl = split(basis[k])
        part = (dot(bh, pick16, 0, 0), dot(bl, pick16, 0, 0))
        total = part if total is None else (total[0] + part[0], total[1] + part[1])
        dh, dl = split(dinv[k])
        if k == 0:
            now = dot(dh, pick16) + dot(dl, pick16)
        else:
            last = (gmat[0, (k - 1) * blk:k * blk, :], gmat[1, (k - 1) * blk:k * blk, :])
            now = dot3((dh, dl), split(pick - dot3(split(coup[k - 1]), last)))
        nh, nl = split(now)
        gmat[0, k * blk:(k + 1) * blk, :] = nh
        gmat[1, k * blk:(k + 1) * blk, :] = nl
    bet[0] = total[0].astype(BF16)
    bet[1] = total[1].astype(BF16)
    bet_now = (bet[0], bet[1])
    bch, bcl = split(dot3(bet_now, split(cinv[...]), 0, 0))
    bc[0] = bch
    bc[1] = bcl
    gnow = (gmat[0], gmat[1])
    sh, sl = split(dot3(gnow, gnow, 0, 0) + dot3((bch, bcl), bet_now))
    smat[0] = sh
    smat[1] = sl

    cm_copy.wait_recv()
    cuts[width:, :] = column(drecv[0:1, :])
    pres[width:, :] = column(drecv[1:2, :])

    exchanges = {}

    def apply(step, c, vec):
        parts = split(vec)
        usend[step, c] = dot3((bet[0], bet[1]), parts)
        ucopies = [
            send(
                usend.at[step, c], urecv.at[step, c, j - 1],
                s_u.at[step, c, j - 1], r_u.at[step, c, j - 1], grp_peer(j),
            )
            for j in range(1, grps)
        ]
        out = dot3((smat[0], smat[1]), parts)
        others = None
        for j, copy in enumerate(ucopies):
            copy.wait_recv()
            others = urecv[step, c, j] if others is None else others + urecv[step, c, j]
        if others is not None:
            out = out + dot3((bc[0], bc[1]), split(others))
        ysend[step, c] = out
        lower, top = pl.ds(width, width), pl.ds(0, width)
        moves = [
            send(
                ysend.at[step, c, lower], yrecv.at[step, c, top],
                s_dn.at[step, c], r_dn.at[step, c], before,
            )
        ]
        if step + 1 < ROUNDS:
            moves.append(
                send(
                    ysend.at[step, c, top], yrecv.at[step, c, lower],
                    s_up.at[step, c], r_up.at[step, c], after,
                )
            )
        exchanges[step, c] = moves
        sent.extend(ucopies + moves)

    def image(step, c):
        for copy in exchanges[step, c]:
            copy.wait_recv()
        if step + 1 < ROUNDS:
            return cuts[...] * (ysend[step, c] + yrecv[step, c])
        return cuts[:width, :] * (ysend[step, c, :width, :] + yrecv[step, c, :width, :])

    def reduce(which):
        copies = [
            send(red.at[which], reda.at[which, j - 1], s_a.at[which, j - 1], r_a.at[which, j - 1], plane_peer(j))
            for j in range(1, plane)
        ]
        total = red[which]
        for j, copy in enumerate(copies):
            copy.wait_recv()
            total = total + reda[which, j]
        sent.extend(copies)
        if outer > 1:
            redm[which] = total
            copies = [
                send(redm.at[which], redb.at[which, j - 1], s_b.at[which, j - 1], r_b.at[which, j - 1], outer_peer(j))
                for j in range(1, outer)
            ]
            for j, copy in enumerate(copies):
                copy.wait_recv()
                total = total + redb[which, j]
            sent.extend(copies)
        return total

    def summed(a, b):
        return jnp.sum(a * b, axis=0, keepdims=True)

    red[...] = jnp.zeros_like(red)
    for c in range(chunks):
        v0_copy[c].wait_recv()
        apply(0, c, v0[c])
    for c in range(chunks):
        w = image(0, c)
        w0[c] = w
        v1 = pres[...] * w
        apply(1, c, v1)
        top = w[:width, :]
        r0 = cuts[:width, :] * rhs[:, col(c)]
        red[0, 0:1, col(c)] = summed(r0, v0[c, :width, :])
        red[0, 1:2, col(c)] = summed(top, v0[c, :width, :])
        red[0, 2:3, col(c)] = summed(top, v1[:width, :])
    first = reduce(0)
    alphas, betas = [], []
    for c in range(chunks):
        m0, m1, m2 = (first[i:i + 1, col(c)] for i in range(3))
        alpha = m0 / m1
        beta = (m0 - 2.0 * alpha * m1 + alpha * alpha * m2) / m0
        alphas.append(alpha)
        betas.append(beta)
        w1 = image(1, c)
        t1 = w0[c] - alpha * w1
        s1 = t1 + beta * w0[c]
        vnext = pres[...] * s1
        apply(2, c, vnext)
        wt = w0[c, :width, :]
        vt = v0[c, :width, :]
        t1, s1, vn = t1[:width, :], s1[:width, :], vnext[:width, :]
        z1 = vt - alpha * (pres[:width, :] * wt)
        r1 = cuts[:width, :] * rhs[:, col(c)] - alpha * wt
        d1 = z1 + beta * vt
        v2[c] = vn
        for i, kept in enumerate((t1, s1, z1, r1, d1)):
            upper[c, i] = kept
        pairs = ((r1, z1), (d1, s1), (s1, z1), (s1, vn), (z1, t1), (vn, t1))
        for i, (a, b) in enumerate(pairs):
            red[1, i:i + 1, col(c)] = summed(a, b)
    for c in range(chunks):
        w2 = image(2, c)
        w0[c, :width, :] = w2
        red[1, 6:7, col(c)] = summed(upper[c, 2], w2)
        red[1, 7:8, col(c)] = summed(v2[c], w2)
    second = reduce(1)
    for c in range(chunks):
        rz1, pi1, sz, sv, zt, vt1, zw, vw = (second[i:i + 1, col(c)] for i in range(8))
        alpha0 = alphas[c]
        alpha1 = rz1 / pi1
        rz2 = rz1 - 2.0 * alpha1 * sz + alpha1 * alpha1 * sv
        beta1 = rz2 / rz1
        pi2 = zt - alpha1 * (zw + vt1) + alpha1 * alpha1 * vw
        pi2 = pi2 + 2.0 * beta1 * (sz - alpha1 * sv) + beta1 * beta1 * pi1
        alpha2 = rz2 / pi2
        t1, s1, z1, r1, d1 = (upper[c, i] for i in range(5))
        d2 = z1 - alpha1 * v2[c] + beta1 * d1
        f2 = t1 - alpha1 * w0[c, :width, :] + beta1 * s1
        mult[:, col(c)] = alpha0 * v0[c, :width, :] + alpha1 * d1 + alpha2 * d2
        resid[:, col(c)] = r1 - alpha1 * s1 - alpha2 * f2
    for copy in sent:
        copy.wait_send()


def local(
    subs, grps,
    rhs_jump, incision, precond, left_rows, right_rows, diag_inv, coupling, coarse_basis, coarse_inv,
):
    width, loads = rhs_jump.shape[2:]
    nblk, blk = diag_inv.shape[2:4]
    primal = coarse_basis.shape[-1]
    order = nblk * blk
    inner = next(n for n in (4, 2, 1) if subs % n == 0)
    outer = subs // inner
    plane = inner * grps
    chunks = 2 if loads % 256 == 0 else 1
    cols = loads // chunks
    others = max(grps - 1, 1)
    dma = pltpu.SemaphoreType.DMA
    vmem = pltpu.VMEM
    scratch = [
        vmem((chunks, 2 * width, cols), F32),
        vmem((chunks, 2 * width, cols), F32),
        vmem((chunks, width, cols), F32),
        vmem((chunks, 5, width, cols), F32),
        vmem((2 * width, cols), F32),
        vmem((2 * width, cols), F32),
        vmem((2, 2 * width, 2 * width), BF16),
        vmem((2, primal, 2 * width), BF16),
        vmem((2, 2 * width, primal), BF16),
        vmem((2, order, 2 * width), BF16),
        vmem((ROUNDS, chunks, 2 * width, cols), F32),
        vmem((ROUNDS, chunks, 2 * width, cols), F32),
        vmem((ROUNDS, chunks, primal, cols), F32),
        vmem((ROUNDS, chunks, others, primal, cols), F32),
        vmem((8, width), F32),
        vmem((8, width), F32),
        vmem((2, 8, loads), F32),
        vmem((2, max(plane - 1, 1), 8, loads), F32),
        vmem((2, max(outer - 1, 1), 8, loads), F32),
        vmem((2, 8, loads), F32),
        dma((chunks,)), dma((chunks,)),
        dma, dma,
        dma((ROUNDS, chunks)), dma((ROUNDS, chunks)),
        dma((ROUNDS, chunks)), dma((ROUNDS, chunks)),
        dma((ROUNDS, chunks, others)), dma((ROUNDS, chunks, others)),
        dma((2, max(plane - 1, 1))), dma((2, max(plane - 1, 1))),
        dma((2, max(outer - 1, 1))), dma((2, max(outer - 1, 1))),
    ]
    shape = jax.ShapeDtypeStruct((width, loads), F32)
    mult, resid = pl.pallas_call(
        functools.partial(kernel, subs, grps, inner, chunks),
        out_shape=(shape, shape),
        in_specs=[pl.BlockSpec(memory_space=pltpu.VMEM)] * 9,
        out_specs=(pl.BlockSpec(memory_space=pltpu.VMEM),) * 2,
        scratch_shapes=scratch,
        compiler_params=pltpu.CompilerParams(
            collective_id=0, has_side_effects=True, vmem_limit_bytes=48 * 1024 * 1024
        ),
    )(
        rhs_jump[0, 0], incision[0], precond[0], left_rows[0], right_rows[0],
        diag_inv[0, 0], coupling[0, 0], coarse_basis[0, 0], coarse_inv[0],
    )
    return mult[None, None], resid[None, None]


def solution(mesh):
    sizes = dict(mesh.shape)
    placed = (
        P("sub", "grp", None, None),
        P("sub", "grp", None),
        P("sub", "grp", None),
        P("sub", "grp", None),
        P("sub", "grp", None),
        P("sub", "grp", None, None, None),
        P("sub", "grp", None, None, None),
        P("sub", "grp", None, None, None),
        P("sub", None, None),
    )
    return jax.shard_map(
        functools.partial(local, sizes["sub"], sizes["grp"]),
        mesh=mesh,
        in_specs=placed,
        out_specs=(P("sub", "grp", None, None), P("sub", "grp", None, None)),
        check_vma=False,
    )
```

time: 367 us -> 77.4 us (0.21); the launches traced: 362 us -> 77.1 us
  blocking collectives: 122 us -> 0 us
  matrix products: 66.7 us -> 0 us
  Pallas kernels: 0 us -> 66.7 us
  waiting for transfers between devices: 61.8 us -> 0 us
  other arithmetic: 50.2 us -> 0 us
  starting transfers between devices: 24.3 us -> 0 us
  between operations: 14.6 us -> 0.66 us
  local copies, waits for them, and re-layouts: 22.8 us -> 9.71 us
    psum x3 -> x0, blocking collectives: 122 us -> none  [pair_totals(): return lax.psum((first, second), ('sub', 'grp'))]
    pallas_call x0 -> x1, Pallas kernels: none -> 66.7 us  [local(): pl.pallas_call(functools.partial(kernel, subs, grps, inner, chunks), out_...]
    dot_general x39 -> x0, matrix products: 66.7 us -> none  [the longest x9 17.9 us: banded(): forward.append(jnp.dot(dinv[block], rhs_now, precision=HIGH))]
    psum x3 -> x0, waiting for transfers between devices: 36.8 us -> none  [interior(): summed = lax.psum(primal, 'grp')]
    ppermute x6 -> x0, waiting for transfers between devices: 24.9 us -> none  [passed_along(): lax.ppermute(shard, axis, [(i, (i + by) % peers) for i in range(peers)])]
    scatter-add x6 -> x0, other arithmetic: 24.9 us -> none  [interior(): load = zeros.at[rrow].add(own).at[lrow].add(-left)]
    ppermute x6 -> x0, starting transfers between devices: 23.8 us -> none  [passed_along(): lax.ppermute(shard, axis, [(i, (i + by) % peers) for i in range(peers)])]
    gather x6 -> x0, local copies, waits for them, and re-layouts: 13.7 us -> none  [interior(): return (jnp.take(disp, lrow, axis=0), jnp.take(disp, rrow, axis=0))]
  transfers between devices with their start and end apart: 9 -> 0, of which waited for: 9 -> 0; matrix products, arithmetic and copies ran while one was open for 9% -> 0% of each run, Pallas kernels for 0% -> 0%
where the time goes in v1:
time: 77.4 us; the launch traced here: 77.1 us
  Pallas kernels  66.7 us (86%)
  local copies, waits for them, and re-layouts  9.71 us (13%)
    pallas_call x1, Pallas kernels, local(): pl.pallas_call(functools.partial(kernel, subs, grps, inner, chunks), out_...  66.7 us
    unnamed x20, local copies, waits for them, and re-layouts  9.71 us

profile of v1, /device:TPU:0, one launch (start us, length us, event | category | flops | bytes accessed | tf_op | source)
XLA Modules:
  0.0 77.1 jit_solution(12124656070945896511)
XLA Ops:
  0.6 0.0 copy-start
  0.6 1.5 %copy-done = f32[1,1,3,384,384]{4,3,2,1,0:T(8,128)S(1)} copy-done((f32[1,1,3,384,384]{4,3,2,1,0:T(8,128)S(1)}, f32[1,1,3,384,384]{4,3,2,1,0:T(8,128)}, u32[]{:S(2)}) %copy-start) | copy-done | bytes 1769496
  2.1 0.0 copy-start.1
  2.1 1.3 %copy-done.1 = f32[1,1,2,384,384]{4,3,2,1,0:T(8,128)S(1)} copy-done((f32[1,1,2,384,384]{4,3,2,1,0:T(8,128)S(1)}, f32[1,1,2,384,384]{4,3,2,1,0:T(8,128)}, u32[]{:S(2)}) %copy-start.1) | copy-done | bytes 1179672
  3.4 0.0 copy-start.2
  3.4 1.1 %copy-done.2 = f32[1,1,3,384,128]{4,3,2,1,0:T(8,128)S(1)} copy-done((f32[1,1,3,384,128]{4,3,2,1,0:T(8,128)S(1)}, f32[1,1,3,384,128]{4,3,2,1,0:T(8,128)}, u32[]{:S(2)}) %copy-start.2) | copy-done | bytes 589848
  4.4 0.0 copy-start.3
  4.4 0.9 %copy-done.3 = f32[1,1,256,256]{3,2,1,0:T(8,128)S(1)} copy-done((f32[1,1,256,256]{3,2,1,0:T(8,128)S(1)}, f32[1,1,256,256]{3,2,1,0:T(8,128)}, u32[]{:S(2)}) %copy-start.3) | copy-done | bytes 262168
  5.4 0.0 copy-start.4
  5.4 0.8 %copy-done.4 = f32[1,128,128]{2,1,0:T(8,128)S(1)} copy-done((f32[1,128,128]{2,1,0:T(8,128)S(1)}, f32[1,128,128]{2,1,0:T(8,128)}, u32[]{:S(2)}) %copy-start.4) | copy-done | bytes 65560
  6.2 0.0 copy-start.5
  6.2 0.7 copy-done.5
  6.9 0.0 copy-start.6
  6.9 0.7 copy-done.6
  7.6 0.0 copy-start.7
  7.6 0.7 copy-done.7
  8.3 0.0 copy-start.8
  8.3 0.7 copy-done.8
  9.0 66.7 %shard_map.104 = (f32[256,256]{1,0:T(8,128)S(1)}, f32[256,256]{1,0:T(8,128)S(1)}) custom-call(f32[256,256]{1,0:T(8,128)S(1)} %bitcast.14, s32[1,256]{1,0:T(1,128)S(1)} %bitcast.18, f32[1,256]{1,0:T(1,128)S(1)} %bitcast.19, s32[1,256]{1,0:T(1,128)S(1)} %bitcast.20, s32[1,256]{1,0:T(1,128)S(1)} %bitcast.21, f32[3,384,384]{2,1,0:T(8,128)S(1)} %bitcast.11, ...), custom_call_target="tpu_custom_call" | custom-call | tf_op jit(solution)/shard_map/pallas_call | solution.py:319
  75.7 0.7 copy.13
  76.4 0.7 copy.14
Async XLA Ops:
  0.6 1.5 %copy-start = (f32[1,1,3,384,384]{4,3,2,1,0:T(8,128)S(1)}, f32[1,1,3,384,384]{4,3,2,1,0:T(8,128)}, u32[]{:S(2)}) copy-start(f32[1,1,3,384,384]{4,3,2,1,0:T(8,128)} %param.14) | copy-start | bytes 5308420
  2.1 1.3 %copy-start.1 = (f32[1,1,2,384,384]{4,3,2,1,0:T(8,128)S(1)}, f32[1,1,2,384,384]{4,3,2,1,0:T(8,128)}, u32[]{:S(2)}) copy-start(f32[1,1,2,384,384]{4,3,2,1,0:T(8,128)} %param.15) | copy-start | bytes 3538948
  3.4 1.1 %copy-start.2 = (f32[1,1,3,384,128]{4,3,2,1,0:T(8,128)S(1)}, f32[1,1,3,384,128]{4,3,2,1,0:T(8,128)}, u32[]{:S(2)}) copy-start(f32[1,1,3,384,128]{4,3,2,1,0:T(8,128)} %param.16) | copy-start | bytes 1769476
  4.4 0.9 %copy-start.3 = (f32[1,1,256,256]{3,2,1,0:T(8,128)S(1)}, f32[1,1,256,256]{3,2,1,0:T(8,128)}, u32[]{:S(2)}) copy-start(f32[1,1,256,256]{3,2,1,0:T(8,128)} %param.9) | copy-start | bytes 786436
  5.4 0.8 %copy-start.4 = (f32[1,128,128]{2,1,0:T(8,128)S(1)}, f32[1,128,128]{2,1,0:T(8,128)}, u32[]{:S(2)}) copy-start(f32[1,128,128]{2,1,0:T(8,128)} %param.17) | copy-start | bytes 196612
  6.2 0.7 copy-start.5
  6.9 0.7 copy-start.6
  7.6 0.7 copy-start.7
  8.3 0.7 copy-start.8

commit v2 on v1

--- a/solution.py
+++ b/solution.py
@@ -29,12 +29,21 @@
 
 def kernel(
     subs, grps, inner, chunks,
-    rhs, cut_in, pre_in, lrow, rrow, dinv, coup, basis, cinv,
-    mult, resid,
-    v0, w0, v2, upper, cuts, pres, smat, bet, bc, gmat,
-    ysend, yrecv, usend, urecv, dsend, drecv, red, reda, redb, redm,
-    s_v0, r_v0, s_cm, r_cm, s_up, r_up, s_dn, r_dn, s_u, r_u, s_a, r_a, s_b, r_b,
+    *refs,
 ):
+    ins, (mult, resid), held = refs[:9], refs[9:11], refs[11:20]
+    s_in = refs[20]
+    (
+        v0, w0, v2, upper, cuts, pres, smat, bet, bc, gmat,
+        ysend, yrecv, usend, urecv, dsend, drecv, red, reda, redb, redm,
+        s_v0, r_v0, s_cm, r_cm, s_up, r_up, s_dn, r_dn, s_u, r_u, s_a, r_a, s_b, r_b,
+    ) = refs[21:]
+    rhs, cut_in, pre_in, lrow, rrow, dinv, coup, basis, cinv = held
+    loads_in = [
+        pltpu.make_async_copy(src, dst, s_in.at[i]) for i, (src, dst) in enumerate(zip(ins, held))
+    ]
+    for copy in loads_in:
+        copy.start()
     sub, grp = lax.axis_index("sub"), lax.axis_index("grp")
     width = rhs.shape[0]
     cols = rhs.shape[1] // chunks
@@ -82,6 +91,8 @@
             jnp.sum(jnp.where(eye, row, 0.0), axis=1, keepdims=True), (width, cols)
         )
 
+    for copy in loads_in[:3]:
+        copy.wait()
     cut_row = cut_in[...].astype(F32)
     dsend[0:1, :] = cut_row
     dsend[1:2, :] = pre_in[...]
@@ -98,6 +109,8 @@
     ]
     sent += [cm_copy] + v0_copy
 
+    for copy in loads_in[3:]:
+        copy.wait()
     index = jnp.concatenate([rrow[...], lrow[...]], axis=1)
     sign = jnp.where(
         lax.broadcasted_iota(jnp.int32, (1, 2 * width), 1) < width, 1.0, -1.0
@@ -286,7 +299,12 @@
     others = max(grps - 1, 1)
     dma = pltpu.SemaphoreType.DMA
     vmem = pltpu.VMEM
-    scratch = [
+    given = (
+        rhs_jump[0, 0], incision[0], precond[0], left_rows[0], right_rows[0],
+        diag_inv[0, 0], coupling[0, 0], coarse_basis[0, 0], coarse_inv[0],
+    )
+    scratch = [vmem(array.shape, array.dtype) for array in given] + [dma((len(given),))]
+    scratch += [
         vmem((chunks, 2 * width, cols), F32),
         vmem((chunks, 2 * width, cols), F32),
         vmem((chunks, width, cols), F32),
@@ -319,16 +337,13 @@
     mult, resid = pl.pallas_call(
         functools.partial(kernel, subs, grps, inner, chunks),
         out_shape=(shape, shape),
-        in_specs=[pl.BlockSpec(memory_space=pltpu.VMEM)] * 9,
+        in_specs=[pl.BlockSpec(memory_space=pl.ANY)] * 9,
         out_specs=(pl.BlockSpec(memory_space=pltpu.VMEM),) * 2,
         scratch_shapes=scratch,
         compiler_params=pltpu.CompilerParams(
-            collective_id=0, has_side_effects=True, vmem_limit_bytes=48 * 1024 * 1024
+            collective_id=0, has_side_effects=True, vmem_limit_bytes=60 * 1024 * 1024
         ),
-    )(
-        rhs_jump[0, 0], incision[0], precond[0], left_rows[0], right_rows[0],
-        diag_inv[0, 0], coupling[0, 0], coarse_basis[0, 0], coarse_inv[0],
-    )
+    )(*given)
     return mult[None, None], resid[None, None]
 
 

time: 77.4 us -> 71.8 us (0.928)
  local copies, waits for them, and re-layouts: 9.71 us -> 3.34 us
  Pallas kernels: 66.7 us -> 67.7 us
    unnamed x20 -> x2, local copies, waits for them, and re-layouts: 9.71 us -> 3.34 us
    pallas_call x1, Pallas kernels: 66.7 us -> 67.7 us  [local(): pl.pallas_call(functools.partial(kernel, subs, grps, inner, chunks), out_...]
where the time goes in v2:
time: 71.8 us; the launch traced here: 71.7 us
  Pallas kernels  67.7 us (94%)
  local copies, waits for them, and re-layouts  3.34 us (5%)
    pallas_call x1, Pallas kernels, local(): pl.pallas_call(functools.partial(kernel, subs, grps, inner, chunks), out_...  67.7 us
    unnamed x2, local copies, waits for them, and re-layouts  3.34 us

profile of v2, /device:TPU:0, one launch (start us, length us, event | category | flops | bytes accessed | tf_op | source)
XLA Modules:
  0.0 71.7 jit_solution(8360843463664786651)
XLA Ops:
  0.6 67.7 %shard_map.104 = (f32[256,256]{1,0:T(8,128)}, f32[256,256]{1,0:T(8,128)}) custom-call(f32[256,256]{1,0:T(8,128)} %bitcast.14, s32[1,256]{1,0:T(1,128)} %bitcast.18, f32[1,256]{1,0:T(1,128)} %bitcast.19, s32[1,256]{1,0:T(1,128)} %bitcast.20, s32[1,256]{1,0:T(1,128)} %bitcast.21, f32[3,384,384]{2,1,0:T(8,128)} %bitcast.11, f32[2,384,384]{2,1,0:T(8,128)} %bitcast.12, ...), custom_call_target="tpu_custom_call" | custom-call | tf_op jit(solution)/shard_map/pallas_call | solution.py:337
  68.3 1.7 %copy.13 = f32[1,1,256,256]{3,2,1,0:T(8,128)} copy(f32[1,1,256,256]{3,2,1,0:T(8,128)} %bitcast.16) | data formatting | bytes 524288
  70.0 1.7 %copy.14 = f32[1,1,256,256]{3,2,1,0:T(8,128)} copy(f32[1,1,256,256]{3,2,1,0:T(8,128)} %bitcast.15) | data formatting | bytes 524288

commit v3 on v2

--- a/solution.py
+++ b/solution.py
@@ -195,16 +195,26 @@
             return cuts[...] * (ysend[step, c] + yrecv[step, c])
         return cuts[:width, :] * (ysend[step, c, :width, :] + yrecv[step, c, :width, :])
 
-    def reduce(which):
-        copies = [
-            send(red.at[which], reda.at[which, j - 1], s_a.at[which, j - 1], r_a.at[which, j - 1], plane_peer(j))
+    begun = {}
+
+    def begin(which, c):
+        here = pl.ds(c * cols, cols)
+        begun[which, c] = [
+            send(
+                red.at[which, :, here], reda.at[which, j - 1, :, here],
+                s_a.at[which, c, j - 1], r_a.at[which, c, j - 1], plane_peer(j),
+            )
             for j in range(1, plane)
         ]
+        sent.extend(begun[which, c])
+
+    def finish(which):
+        for c in range(chunks):
+            for copy in begun[which, c]:
+                copy.wait_recv()
         total = red[which]
-        for j, copy in enumerate(copies):
-            copy.wait_recv()
+        for j in range(plane - 1):
             total = total + reda[which, j]
-        sent.extend(copies)
         if outer > 1:
             redm[which] = total
             copies = [
@@ -228,13 +238,14 @@
         w = image(0, c)
         w0[c] = w
         v1 = pres[...] * w
-        apply(1, c, v1)
         top = w[:width, :]
         r0 = cuts[:width, :] * rhs[:, col(c)]
         red[0, 0:1, col(c)] = summed(r0, v0[c, :width, :])
         red[0, 1:2, col(c)] = summed(top, v0[c, :width, :])
         red[0, 2:3, col(c)] = summed(top, v1[:width, :])
-    first = reduce(0)
+        begin(0, c)
+        apply(1, c, v1)
+    first = finish(0)
     alphas, betas = [], []
     for c in range(chunks):
         m0, m1, m2 = (first[i:i + 1, col(c)] for i in range(3))
@@ -264,7 +275,8 @@
         w0[c, :width, :] = w2
         red[1, 6:7, col(c)] = summed(upper[c, 2], w2)
         red[1, 7:8, col(c)] = summed(v2[c], w2)
-    second = reduce(1)
+        begin(1, c)
+    second = finish(1)
     for c in range(chunks):
         rz1, pi1, sz, sv, zt, vt1, zw, vw = (second[i:i + 1, col(c)] for i in range(8))
         alpha0 = alphas[c]
@@ -330,7 +342,7 @@
         dma((ROUNDS, chunks)), dma((ROUNDS, chunks)),
         dma((ROUNDS, chunks)), dma((ROUNDS, chunks)),
         dma((ROUNDS, chunks, others)), dma((ROUNDS, chunks, others)),
-        dma((2, max(plane - 1, 1))), dma((2, max(plane - 1, 1))),
+        dma((2, chunks, max(plane - 1, 1))), dma((2, chunks, max(plane - 1, 1))),
         dma((2, max(outer - 1, 1))), dma((2, max(outer - 1, 1))),
     ]
     shape = jax.ShapeDtypeStruct((width, loads), F32)

time: 71.8 us -> 65.7 us (0.915)
  Pallas kernels: 67.7 us -> 61.5 us
    pallas_call x1, Pallas kernels: 67.7 us -> 61.5 us  [local(): pl.pallas_call(functools.partial(kernel, subs, grps, inner, chunks), out_...]
where the time goes in v3:
time: 65.7 us; the launch traced here: 65.5 us
  Pallas kernels  61.5 us (94%)
  local copies, waits for them, and re-layouts  3.34 us (5%)
    pallas_call x1, Pallas kernels, local(): pl.pallas_call(functools.partial(kernel, subs, grps, inner, chunks), out_...  61.5 us
    unnamed x2, local copies, waits for them, and re-layouts  3.34 us

profile of v3, /device:TPU:0, one launch (start us, length us, event | category | flops | bytes accessed | tf_op | source)
XLA Modules:
  0.0 65.5 jit_solution(3898936959525339593)
XLA Ops:
  0.6 61.5 %shard_map.104 = (f32[256,256]{1,0:T(8,128)}, f32[256,256]{1,0:T(8,128)}) custom-call(f32[256,256]{1,0:T(8,128)} %bitcast.14, s32[1,256]{1,0:T(1,128)} %bitcast.18, f32[1,256]{1,0:T(1,128)} %bitcast.19, s32[1,256]{1,0:T(1,128)} %bitcast.20, s32[1,256]{1,0:T(1,128)} %bitcast.21, f32[3,384,384]{2,1,0:T(8,128)} %bitcast.11, f32[2,384,384]{2,1,0:T(8,128)} %bitcast.12, ...), custom_call_target="tpu_custom_call" | custom-call | tf_op jit(solution)/shard_map/pallas_call | solution.py:349
  62.1 1.7 %copy.13 = f32[1,1,256,256]{3,2,1,0:T(8,128)} copy(f32[1,1,256,256]{3,2,1,0:T(8,128)} %bitcast.16) | data formatting | bytes 524288
  63.8 1.7 %copy.14 = f32[1,1,256,256]{3,2,1,0:T(8,128)} copy(f32[1,1,256,256]{3,2,1,0:T(8,128)} %bitcast.15) | data formatting | bytes 524288
